TPU v7x, 32 devices: a whole 2x2x4 slice. The times are simulated.
32 devices in a mesh: ch: 16 (over z, y, core), ta: 2 (over x).
Axes of the slice: x: 2, y: 2, z: 4, core: 2. Of those that a mesh axis runs over, the one named last changes fastest.
Arguments:
- templates: bfloat16 [64, 200, 8192], P('ta', None, 'ch')
- record: float32 [8192, 512], P('ch', 'ta')
- record_tail: float32 [8192, 199], P('ch')
Outputs:
- stacked: float32 [64, 512], P('ch', 'ta')
All inputs are finite; a program needn't handle non-finite values.
Results may differ from a plain program's by a relative error of at most 0.00044.
Values may be sent and summed in bfloat16 or wider, within the bound.
A program may use at most 128 MiB of HBM per device.

v0:
```python
import math

import jax
import jax.numpy as jnp
from jax import lax
from jax.sharding import PartitionSpec as P

C = 8192


def normalize(templates):
    samples = templates.shape[1]
    values = templates.astype(jnp.float32)
    centred = values - jnp.mean(values, axis=1, keepdims=True)
    scaled = (
        centred
        * lax.rsqrt(jnp.mean(centred * centred, axis=1, keepdims=True) + 1e-06)
        / math.sqrt(samples)
    )
    return scaled.astype(jnp.bfloat16)


def sliding_stats(full_trace, samples, lag_count):
    centre = jnp.mean(full_trace, axis=1, keepdims=True)
    shifted = full_trace - centre
    zero_column = jnp.zeros((full_trace.shape[0], 1), jnp.float32)
    first_sum = jnp.concatenate([zero_column, jnp.cumsum(shifted, axis=1)], axis=1)
    second_sum = jnp.concatenate([zero_column, jnp.cumsum(shifted * shifted, axis=1)], axis=1)
    mean_shift = (first_sum[:, samples : samples + lag_count] - first_sum[:, :lag_count]) / samples
    window_var = (
        second_sum[:, samples : samples + lag_count] - second_sum[:, :lag_count]
    ) / samples - mean_shift * mean_shift
    scale = lax.rsqrt(jnp.maximum(window_var, 0.0) + 1e-06) / math.sqrt(samples)
    return (mean_shift + centre, scale)


def correlate(normed, full_trace, lag_count):
    samples = normed.shape[1]
    channels = full_trace.shape[0]
    target = max(1, (1 << 22) // (samples * lag_count))
    target = 1 << target.bit_length() - 1
    block_rows = math.gcd(channels, target)
    window_mean, scale = sliding_stats(full_trace, samples, lag_count)

    def advance(block_index, running):
        first_row = block_index * block_rows
        channel_rows = lax.dynamic_slice_in_dim(full_trace, first_row, block_rows, 0)
        mean_rows = lax.dynamic_slice_in_dim(window_mean, first_row, block_rows, 0)
        scale_rows = lax.dynamic_slice_in_dim(scale, first_row, block_rows, 0)
        hankel = jnp.stack(
            [channel_rows[:, offset : offset + lag_count] for offset in range(samples)], axis=1
        )
        windows = ((hankel - mean_rows[:, None, :]) * scale_rows[:, None, :]).astype(jnp.bfloat16)
        unit_part = lax.dynamic_slice_in_dim(normed, first_row, block_rows, 2)
        return running + lax.dot_general(
            unit_part, windows, (((1, 2), (1, 0)), ((), ())), preferred_element_type=jnp.float32
        )

    initial = jnp.zeros((normed.shape[0], lag_count), jnp.float32)
    return lax.fori_loop(0, channels // block_rows, advance, initial)


def on_device(templates, record, record_tail):
    normed = normalize(templates)
    unit_all = lax.all_to_all(normed, "ta", split_axis=2, concat_axis=0, tiled=True)
    full_time = lax.all_to_all(record, "ta", split_axis=0, concat_axis=1, tiled=True)
    per_group = full_time.shape[0]
    tail_rows = lax.dynamic_slice_in_dim(
        record_tail, lax.axis_index("ta") * per_group, per_group, 0
    )
    extended = jnp.concatenate([full_time, tail_rows], axis=1)
    partial_value = correlate(unit_all, extended, full_time.shape[1])
    n_chan = lax.axis_size("ch")
    n_time = lax.axis_size("ta")
    count_all = partial_value.shape[0]
    lag_dev = partial_value.shape[1] // n_time
    arranged = (
        partial_value.reshape(n_chan, count_all // n_chan, n_time, lag_dev)
        .transpose(0, 2, 1, 3)
        .reshape(n_chan * n_time, count_all // n_chan, lag_dev)
    )
    stacked = lax.psum_scatter(arranged, ("ch", "ta"), scatter_dimension=0, tiled=True)[0]
    return stacked * (1.0 / C)


def solution(mesh):
    return jax.shard_map(
        on_device,
        mesh=mesh,
        in_specs=(P("ta", None, "ch"), P("ch", "ta"), P("ch", None)),
        out_specs=P("ch", "ta"),
        check_vma=False,
    )
```

profile of v0, /device:TPU:0, one launch (start us, length us, event | category | flops | bytes accessed | tf_op | source)
XLA Modules:
  0.0 1582.8 jit_solution(12593468454031995062)
XLA Ops:
  6.5 2.0 copy.25
  8.6 4.2 all-to-all-start.1
  12.8 14.3 copy.23
  27.0 5.8 convert_reduce_fusion
  32.9 13.5 fusion.12
  46.5 7.1 fusion.14
  53.5 6.9 all-to-all-start
  61.9 0.9 slice.1645
  64.0 1.6 fusion.27
  66.3 87.3 %all-to-all-done = bf16[32,200,512]{1,0,2:T(8,128)(2,1)} async-done(((bf16[32,200,512]{1,0,2:T(8,128)(2,1)}), bf16[32,200,512]{1,0,2:T(8,128)(2,1)}, u32[]{:S(2)}, u32[]{:S(2)}) %all-to-all-start) | async-done | bytes 6553632 | tf_op jit(solution)/shard_map/all_to_all | solution.py:65
  153.6 8.1 copy.24
  161.7 1289.1 %while.14 = (s32[]{:T(128)}, f32[64,512]{1,0:T(8,128)S(1)}, bf16[64,200,256]{1,0,2:T(8,128)(2,1)}, f32[256,711]{1,0:T(8,128)S(1)}, f32[256,512]{1,0:T(8,128)S(1)...) while((s32[]{:T(128)}, f32[64,512]{1,0:T(8,128)S(1)}, ...), condition=%wide.region_9.10_spmd.clone, body=%wide.region_8.9_spmd.clone.sunk | while | flops 429326528 | bytes 54138476 | solution.py:60
  172.2 0.7 constant_dynamic-update-slice_fusion.415
  191.9 0.7 constant_dynamic-update-slice_fusion.443
  206.8 0.7 constant_dynamic-update-slice_fusion.464
  296.3 0.7 constant_dynamic-update-slice_fusion.591
  302.7 9.6 multiply_convert_fusion.2
  312.3 10.5 fusion.36
  333.3 0.7 constant_dynamic-update-slice_fusion.415
  353.1 0.7 constant_dynamic-update-slice_fusion.443
  367.9 0.7 constant_dynamic-update-slice_fusion.464
  457.5 0.7 constant_dynamic-update-slice_fusion.591
  463.9 9.6 multiply_convert_fusion.2
  473.4 10.5 fusion.36
  494.5 0.7 constant_dynamic-update-slice_fusion.415
  514.2 0.7 constant_dynamic-update-slice_fusion.443
  529.1 0.7 constant_dynamic-update-slice_fusion.464
  618.6 0.7 constant_dynamic-update-slice_fusion.591
  625.0 9.6 multiply_convert_fusion.2
  634.6 10.5 fusion.36
  655.6 0.7 constant_dynamic-update-slice_fusion.415
  675.4 0.7 constant_dynamic-update-slice_fusion.443
  690.2 0.7 constant_dynamic-update-slice_fusion.464
  779.7 0.7 constant_dynamic-update-slice_fusion.591
  786.1 9.6 multiply_convert_fusion.2
  795.7 10.5 fusion.36
  816.7 0.7 constant_dynamic-update-slice_fusion.415
  836.5 0.7 constant_dynamic-update-slice_fusion.443
  851.3 0.7 constant_dynamic-update-slice_fusion.464
  895.8 0.7 constant_dynamic-update-slice_fusion.527
  940.9 0.7 constant_dynamic-update-slice_fusion.591
  947.3 9.6 multiply_convert_fusion.2
  956.8 10.5 fusion.36
  977.9 0.7 constant_dynamic-update-slice_fusion.415
  997.6 0.7 constant_dynamic-update-slice_fusion.443
  1012.5 0.7 constant_dynamic-update-slice_fusion.464
  1056.9 0.7 constant_dynamic-update-slice_fusion.527
  1102.0 0.7 constant_dynamic-update-slice_fusion.591
  1108.4 9.6 multiply_convert_fusion.2
  1118.0 10.5 fusion.36
  1139.0 0.7 constant_dynamic-update-slice_fusion.415
  1158.8 0.7 constant_dynamic-update-slice_fusion.443
  1173.6 0.7 constant_dynamic-update-slice_fusion.464
  1263.2 0.7 constant_dynamic-update-slice_fusion.591
  1269.5 9.6 multiply_convert_fusion.2
  1279.1 10.5 fusion.36
  1300.1 0.7 constant_dynamic-update-slice_fusion.415
  1319.9 0.7 constant_dynamic-update-slice_fusion.443
  1334.7 0.7 constant_dynamic-update-slice_fusion.464
  1424.3 0.7 constant_dynamic-update-slice_fusion.591
  1430.7 9.6 multiply_convert_fusion.2
  1440.3 10.5 fusion.36
  1451.5 123.1 %all-reduce.7.cloned.1.call-done = f32[32,4,256]{2,1,0:T(4,128)} async-done(((f32[32,4,256]{2,1,0:T(4,128)}), f32[32,4,256]{2,1,0:T(4,128)}) %all-reduce.7.cloned.1.call-update) | async-done | bytes 131088
  1574.7 1.3 fusion.28
  (1606 shorter events, 1107.2 us)
Async XLA Ops:
  8.6 45.0 %all-to-all-start.1 = ((f32[2,256,256]{1,2,0:T(8,128)}), f32[2,256,256]{1,2,0:T(8,128)S(1)}, u32[]{:S(2)}, u32[]{:S(2)}) async-start(f32[2,256,256]{1,2,0:T(8,128)} %copy.25), calls=%async_computation.1 | async-start | bytes 1048576 | tf_op jit(solution)/shard_map/all_to_all | solution.py:66
  27.0 5.8 copy-start
  46.4 14.1 copy-start.1
  53.5 100.1 %all-to-all-start = ((bf16[32,200,512]{1,0,2:T(8,128)(2,1)}), bf16[32,200,512]{1,0,2:T(8,128)(2,1)}, u32[]{:S(2)}, u32[]{:S(2)}) async-start(bf16[32,200,512]{1,0,2:T(8,128)(2,1)} %fusion.14), calls=%async_computation | async-start | bytes 16777216 | tf_op jit(solution)/shard_map/all_to_all | solution.py:65
  60.5 1514.2 %all-reduce.7.cloned.1.call-start = ((), (), s32[]{:S(2)}) async-start(), calls=%async_computation.2 | async-start | bytes 262144
Sparse Core Ops, SparseCore 0:
  1451.7 122.9 all-reduce.6
where the time goes:
time: 1580 us
  local copies, waits for them, and re-layouts  1160 us (73%)
  waiting for transfers between devices  210 us (13%)
  other arithmetic  108 us (7%)
  matrix products  83.7 us (5%)
    while x1592, local copies, waits for them, and re-layouts  1120 us
    unnamed x2, waiting for transfers between devices  123 us
    all_to_all x1, waiting for transfers between devices, on_device(): lax.all_to_all(normed, 'ta', split_axis=2, concat_axis=0, tiled=True)  87.3 us
    dot_general x8, matrix products, advance(): lax.dot_general(unit_part, windows, (((1, 2), (1, 0)), ((), ())), preferr...  83.7 us
    convert_element_type x8, other arithmetic, advance(): ((hankel - mean_rows[:, None, :]) * scale_rows[:, None, :]).astype(jnp.bf...  76.6 us
  transfers between devices with their start and end apart: 3, of which 2 were waited for; matrix products, arithmetic and copies ran while one was open for 3% of the time, Pallas kernels for 0%

commit v1 on v0

v1 whole, which is shorter than its diff:
```python
import functools
import math

import jax
import jax.numpy as jnp
from jax import lax
from jax.experimental import pallas as pl
from jax.experimental.pallas import tpu as pltpu
from jax.sharding import PartitionSpec as P

LANES = 128
SHIFTS = 8
VMEM_LIMIT = 56 * 1024 * 1024


def normalize_kernel(t_ref, u_ref, wide):
    rows, samples, _ = t_ref.shape

    def one(k, carry):
        values = t_ref[k].astype(jnp.float32)
        centred = values - jnp.mean(values, axis=0, keepdims=True)
        power = jnp.mean(centred * centred, axis=0, keepdims=True)
        wide[pl.ds(k, samples, stride=rows), :] = centred * (
            lax.rsqrt(power + 1e-06) * (1.0 / math.sqrt(samples))
        )
        return carry

    lax.fori_loop(0, rows, one, 0)

    def cast(m, carry):
        u_ref[0, m] = wide[pl.ds(pl.multiple_of(m * rows, rows), rows), :].astype(jnp.bfloat16)
        return carry

    lax.fori_loop(0, samples, cast, 0)


def normalize(templates, tile):
    count, samples, channels = templates.shape
    rows = math.gcd(count, 16)
    per_tile = tile // LANES
    return pl.pallas_call(
        normalize_kernel,
        grid=(channels // tile, per_tile, count // rows),
        in_specs=[pl.BlockSpec((rows, samples, LANES), lambda i, h, r: (r, 0, i * per_tile + h))],
        out_specs=pl.BlockSpec((1, samples, rows, LANES), lambda i, h, r: (i, 0, r, h)),
        out_shape=jax.ShapeDtypeStruct((channels // tile, samples, count, tile), jnp.bfloat16),
        scratch_shapes=[pltpu.VMEM((samples * rows, LANES), jnp.float32)],
        compiler_params=pltpu.CompilerParams(vmem_limit_bytes=VMEM_LIMIT),
        name="normalize_templates",
    )(templates)


def merge(left, right, n_left, n_right):
    (a0, v0), (a1, v1) = left, right
    w1 = n_right / (n_left + n_right)
    w0 = 1.0 - w1
    gap = a1 - a0
    return (a0 + w1 * gap, w0 * v0 + w1 * v1 + (w0 * w1) * (gap * gap))


def window_stats(x, samples, lag_count):
    mean, var, length = x, jnp.zeros_like(x), 1
    total, done = None, 0
    while True:
        if samples & length:
            piece = (mean[done : done + lag_count], var[done : done + lag_count])
            total = piece if total is None else merge(total, piece, done, length)
            done += length
        if 2 * length > samples:
            return total
        keep = mean.shape[0] - length
        mean, var = merge(
            (mean[:keep], var[:keep]), (mean[length:], var[length:]), length, length
        )
        length *= 2


def correlate_kernel(steps, groups, blocks, x_ref, u_ref, out_ref, xs, mu, rs, w_even, w_odd, acc):
    step = pl.program_id(0)
    rows = w_even.shape[0]
    tile = x_ref.shape[1]
    lag_count = mu.shape[0]
    samples = groups * SHIFTS
    reach = xs.shape[1]
    now = jnp.minimum(step, steps - 1)
    before = jnp.maximum(step - 1, 0)
    block_now = lax.rem(now // groups, blocks)
    block_before = lax.rem(before // groups, blocks)
    first_row = pl.multiple_of(block_now * rows, rows)
    x_row = first_row + lax.rem(now, groups) * SHIFTS

    @pl.when(step == 0)
    def _():
        acc[...] = jnp.zeros_like(acc)
        w_odd[...] = jnp.zeros_like(w_odd)

    @pl.when(lax.rem(step, groups * blocks) == 0)
    def _():
        x = x_ref[...]
        mean, var = window_stats(x, samples, lag_count)
        mu[...] = mean
        rs[...] = lax.rsqrt(var + 1e-06) * (1.0 / math.sqrt(samples))
        for j in range(SHIFTS):
            xs[j] = x[j : j + reach]

    def work(w_now, w_before):
        chunk = math.gcd(rows, 32)
        weights = jnp.concatenate([u_ref[0, j] for j in range(SHIFTS)], axis=1)
        acc_rows = pl.ds(pl.multiple_of(block_before * rows, rows), rows)
        acc[acc_rows, :] += lax.dot_general(
            w_before[...], weights, (((1,), (1,)), ((), ())), preferred_element_type=jnp.float32
        )
        for r in range(0, rows, chunk):
            mean = mu[pl.ds(first_row + r, chunk), :]
            scale = rs[pl.ds(first_row + r, chunk), :]
            for j in range(SHIFTS):
                values = xs[j, pl.ds(pl.multiple_of(x_row + r, 8), chunk), :]
                w_now[pl.ds(r, chunk), pl.ds(j * tile, tile)] = (
                    (values - mean) * scale
                ).astype(jnp.bfloat16)

    @pl.when(lax.rem(step, 2) == 0)
    def _():
        work(w_even, w_odd)

    @pl.when(lax.rem(step, 2) == 1)
    def _():
        work(w_odd, w_even)

    @pl.when(step == steps)
    def _():
        out_ref[...] = acc[...]


def correlate(unit, trace, lag_count):
    tiles, samples, count, tile = unit.shape
    span = trace.shape[0]
    groups = samples // SHIFTS
    rows = math.gcd(lag_count, 512)
    blocks = lag_count // rows
    steps = tiles * blocks * groups
    per_tile = blocks * groups
    reach = lag_count + samples - SHIFTS
    return pl.pallas_call(
        functools.partial(correlate_kernel, steps, groups, blocks),
        grid=(steps + 1,),
        in_specs=[
            pl.BlockSpec((span, tile), lambda s: (0, jnp.minimum(s, steps - 1) // per_tile)),
            pl.BlockSpec(
                (1, SHIFTS, count, tile),
                lambda s: (
                    jnp.maximum(s - 1, 0) // per_tile,
                    lax.rem(jnp.maximum(s - 1, 0), groups),
                    0,
                    0,
                ),
            ),
        ],
        out_specs=pl.BlockSpec((lag_count, count), lambda s: (0, 0)),
        out_shape=jax.ShapeDtypeStruct((lag_count, count), jnp.float32),
        scratch_shapes=[
            pltpu.VMEM((SHIFTS, reach, tile), jnp.float32),
            pltpu.VMEM((lag_count, tile), jnp.float32),
            pltpu.VMEM((lag_count, tile), jnp.float32),
            pltpu.VMEM((rows, SHIFTS * tile), jnp.bfloat16),
            pltpu.VMEM((rows, SHIFTS * tile), jnp.bfloat16),
            pltpu.VMEM((lag_count, count), jnp.float32),
        ],
        compiler_params=pltpu.CompilerParams(vmem_limit_bytes=VMEM_LIMIT),
        name="correlate_windows",
    )(trace, unit)


def on_device(templates, record, record_tail):
    n_chan = lax.axis_size("ch")
    n_time = lax.axis_size("ta")
    tile = math.gcd(record.shape[0], 2 * LANES)
    unit = normalize(templates, tile)
    own = jnp.transpose(record)
    full_time = lax.all_gather(own, "ta", axis=0, tiled=True)
    trace = jnp.concatenate([full_time, jnp.transpose(record_tail)], axis=0)
    lag_count = full_time.shape[0]
    partial_value = jnp.transpose(correlate(unit, trace, lag_count))
    here = partial_value.shape[0]
    count_all = here * n_time
    lag_dev = lag_count // n_time
    placed = lax.dynamic_update_slice(
        jnp.zeros((count_all, lag_count), jnp.float32),
        partial_value,
        (lax.axis_index("ta") * here, 0),
    )
    arranged = (
        placed.reshape(n_chan, count_all // n_chan, n_time, lag_dev)
        .transpose(0, 2, 1, 3)
        .reshape(n_chan * n_time, count_all // n_chan, lag_dev)
    )
    stacked = lax.psum_scatter(arranged, ("ch", "ta"), scatter_dimension=0, tiled=True)[0]
    return stacked * (1.0 / (n_chan * record.shape[0]))


def solution(mesh):
    return jax.shard_map(
        on_device,
        mesh=mesh,
        in_specs=(P("ta", None, "ch"), P("ch", "ta"), P("ch", None)),
        out_specs=P("ch", "ta"),
        check_vma=False,
    )
```

time: 1580 us -> 242 us (0.15)
  local copies, waits for them, and re-layouts: 1160 us -> 3.89 us
  other arithmetic: 108 us -> 3.72 us
  Pallas kernels: 0 us -> 95.5 us
  waiting for transfers between devices: 210 us -> 125 us
  matrix products: 83.7 us -> 0 us
    while x1592 -> x0, local copies, waits for them, and re-layouts: 1120 us -> none
    pallas_call x0 -> x2, Pallas kernels: none -> 95.5 us  [the longest x1 65.7 us: correlate(): pl.pallas_call(functools.partial(correlate_kernel, steps, groups, blocks)...]
    all_to_all x2 -> x0, waiting for transfers between devices: 87.3 us -> none  [the longest x1 87.3 us: on_device(): lax.all_to_all(normed, 'ta', split_axis=2, concat_axis=0, tiled=True)]
    convert_element_type x9 -> x0, other arithmetic: 83.7 us -> none  [the longest x8 76.6 us: advance(): ((hankel - mean_rows[:, None, :]) * scale_rows[:, None, :]).astype(jnp.bf...]
    dot_general x8 -> x0, matrix products: 83.7 us -> none  [advance(): lax.dot_general(unit_part, windows, (((1, 2), (1, 0)), ((), ())), preferr...]
    reduce_sum x4 -> x0, other arithmetic: 19.4 us -> none  [the longest x1 13.5 us: normalize(): jnp.mean(centred * centred, axis=1, keepdims=True) + 1e-06]
    unnamed x2 -> x3, waiting for transfers between devices: 123 us -> 125 us
  transfers between devices with their start and end apart: 3 -> 2, of which waited for: 2 -> 1; matrix products, arithmetic and copies ran while one was open for 3% -> 0% of each run, Pallas kernels for 0% -> 12%
where the time goes in v1:
time: 242 us
  waiting for transfers between devices  125 us (52%)
  Pallas kernels  95.5 us (39%)
  between operations  13.4 us (6%)
  local copies, waits for them, and re-layouts  3.89 us (2%)
  other arithmetic  3.72 us (2%)
    unnamed x3, waiting for transfers between devices  125 us
    pallas_call x1, Pallas kernels, correlate(): pl.pallas_call(functools.partial(correlate_kernel, steps, groups, blocks)...  65.7 us
    pallas_call x1, Pallas kernels, normalize(): pl.pallas_call(normalize_kernel, grid=(channels // tile, per_tile, count...  29.8 us
  transfers between devices with their start and end apart: 2, of which 1 were waited for; matrix products, arithmetic and copies ran while one was open for 0% of the time, Pallas kernels for 12%

profile of v1, /device:TPU:0, one launch (start us, length us, event | category | flops | bytes accessed | tf_op | source)
XLA Modules:
  0.0 241.8 jit_solution(12059018113400287438)
XLA Ops:
  6.5 0.0 all-gather.2.cloned.1.call-start
  6.5 2.0 copy.10
  8.6 0.0 all-gather.2.cloned.1.call-update
  8.6 0.0 all-reduce.3.cloned.1.call-start
  8.7 0.0 copy-start
  8.7 29.8 %normalize_templates.1.u_ref = bf16[2,200,32,256]{3,2,1,0:T(8,128)(2,1)} custom-call(bf16[32,200,512]{2,1,0:T(8,128)(2,1)} %t_ref.1), custom_call_target="tpu_custom_call" | custom-call | tf_op jit(solution)/shard_map/normalize_templates/pallas_call | solution.py:41
  38.4 0.0 all-gather.2.cloned.1.call-done
  38.4 0.0 copy-done
  38.4 2.5 %pad_maximum_fusion.x_ref = f32[711,512]{1,0:T(8,128)} fusion(f32[199,512]{1,0:T(8,128)S(1)} %bitcast.11, f32[512,512]{1,0:T(8,128)} %all-gather.2.cloned.1.call-done), kind=kLoop, calls=%fused_computation | loop fusion | flops 364032 | bytes 2912256 | tf_op jit(solution)/shard_map/concatenate | solution.py:181
  40.9 65.7 %correlate_windows.1 = f32[512,32]{1,0:T(8,128)} custom-call(f32[711,512]{1,0:T(8,128)} %pad_maximum_fusion.x_ref, bf16[2,200,32,256]{3,2,1,0:T(8,128)(2,1)} %normalize_templates.1.u_ref), custom_call_target="tpu_custom_call" | custom-call | tf_op jit(solution)/shard_map/correlate_windows/pallas_call | solution.py:144
  106.6 1.0 copy.11
  107.7 0.1 reshape.8
  107.8 0.7 copy.12
  108.5 0.0 all-reduce.3.cloned.1.call-update
  108.5 125.2 %all-reduce.3.cloned.1.call-done = f32[32,4,256]{2,1,0:T(4,128)} async-done(((f32[32,4,256]{2,1,0:T(4,128)}), f32[32,4,256]{2,1,0:T(4,128)}) %all-reduce.3.cloned.1.call-update) | async-done | bytes 131088
  233.7 1.3 fusion
  (2 shorter events, 0.0 us)
Async XLA Ops:
  6.5 31.9 %all-gather.2.cloned.1.call-start = ((), (), s32[]{:S(2)}) async-start(), calls=%async_computation | async-start | bytes 1572864 | tf_op jit(solution)/shard_map/all_gather | solution.py:180
  8.6 225.1 %all-reduce.3.cloned.1.call-start = ((), (), s32[]{:S(2)}) async-start(), calls=%async_computation.1 | async-start | bytes 262144
  8.7 29.8 %copy-start = (f32[512,199]{0,1:T(8,128)S(1)}, f32[512,199]{0,1:T(8,128)}, u32[]{:S(2)}) copy-start(f32[512,199]{0,1:T(8,128)} %param.5) | copy-start | bytes 1222660
Sparse Core Ops, SparseCore 0:
  8.9 23.9 all-gather.1
  108.6 125.0 all-reduce.2

commit v2 on v1

--- a/solution.py
+++ b/solution.py
@@ -25,13 +25,15 @@
         )
         return carry
 
-    lax.fori_loop(0, rows, one, 0)
-
-    def cast(m, carry):
-        u_ref[0, m] = wide[pl.ds(pl.multiple_of(m * rows, rows), rows), :].astype(jnp.bfloat16)
+    lax.fori_loop(0, rows, one, 0, unroll=4)
+
+    def cast(i, carry):
+        first = i * SHIFTS
+        part = wide[pl.ds(pl.multiple_of(first * rows, 8), SHIFTS * rows), :]
+        u_ref[0, pl.ds(first, SHIFTS)] = part.reshape(SHIFTS, rows, LANES).astype(jnp.bfloat16)
         return carry
 
-    lax.fori_loop(0, samples, cast, 0)
+    lax.fori_loop(0, samples // SHIFTS, cast, 0, unroll=5)
 
 
 def normalize(templates, tile):
@@ -106,9 +108,9 @@
     def work(w_now, w_before):
         chunk = math.gcd(rows, 32)
         weights = jnp.concatenate([u_ref[0, j] for j in range(SHIFTS)], axis=1)
-        acc_rows = pl.ds(pl.multiple_of(block_before * rows, rows), rows)
-        acc[acc_rows, :] += lax.dot_general(
-            w_before[...], weights, (((1,), (1,)), ((), ())), preferred_element_type=jnp.float32
+        acc_lags = pl.ds(pl.multiple_of(block_before * rows, rows), rows)
+        acc[:, acc_lags] += lax.dot_general(
+            weights, w_before[...], (((1,), (1,)), ((), ())), preferred_element_type=jnp.float32
         )
         for r in range(0, rows, chunk):
             mean = mu[pl.ds(first_row + r, chunk), :]
@@ -156,19 +158,115 @@
                 ),
             ),
         ],
-        out_specs=pl.BlockSpec((lag_count, count), lambda s: (0, 0)),
-        out_shape=jax.ShapeDtypeStruct((lag_count, count), jnp.float32),
+        out_specs=pl.BlockSpec((count, lag_count), lambda s: (0, 0)),
+        out_shape=jax.ShapeDtypeStruct((count, lag_count), jnp.float32),
         scratch_shapes=[
             pltpu.VMEM((SHIFTS, reach, tile), jnp.float32),
             pltpu.VMEM((lag_count, tile), jnp.float32),
             pltpu.VMEM((lag_count, tile), jnp.float32),
             pltpu.VMEM((rows, SHIFTS * tile), jnp.bfloat16),
             pltpu.VMEM((rows, SHIFTS * tile), jnp.bfloat16),
-            pltpu.VMEM((lag_count, count), jnp.float32),
+            pltpu.VMEM((count, lag_count), jnp.float32),
         ],
         compiler_params=pltpu.CompilerParams(vmem_limit_bytes=VMEM_LIMIT),
         name="correlate_windows",
     )(trace, unit)
+
+
+def sum_kernel(scale, part_ref, out_ref, outgoing, arrived, send_sem, recv_sem):
+    n_chan, n_time = lax.axis_size("ch"), lax.axis_size("ta")
+    chan, time = lax.axis_index("ch"), lax.axis_index("ta")
+    owners = n_chan // n_time
+    block, lags = out_ref.shape
+    giver = chan // owners
+    own = giver == time
+
+    barrier = pltpu.get_barrier_semaphore()
+    for i in range(n_chan):
+
+        @pl.when(jnp.logical_not(own & (chan == i)))
+        def _():
+            pl.semaphore_signal(
+                barrier, inc=1, device_id=(i, giver), device_id_type=pl.DeviceIdType.MESH
+            )
+
+    for r in range(owners):
+        for b in range(n_time):
+            outgoing[r * n_time + b] = part_ref[
+                pl.ds(r * block, block), pl.ds(b * lags, lags)
+            ]
+    pl.semaphore_wait(barrier, owners * n_time - own.astype(jnp.int32))
+
+    def copy(slot, r, b):
+        return pltpu.make_async_remote_copy(
+            src_ref=outgoing.at[slot],
+            dst_ref=arrived.at[chan],
+            send_sem=send_sem.at[slot],
+            recv_sem=recv_sem.at[chan],
+            device_id=(time * owners + r, b),
+            device_id_type=pl.DeviceIdType.MESH,
+        )
+
+    for r in range(owners):
+        for b in range(n_time):
+            slot = r * n_time + b
+            mine = (time * owners + r == chan) & (time == b)
+
+            @pl.when(jnp.logical_not(mine))
+            def _():
+                copy(slot, r, b).start()
+
+            @pl.when(mine)
+            def _():
+                arrived[chan] = outgoing[slot]
+
+    for i in range(n_chan):
+
+        @pl.when(jnp.logical_not(own & (chan == i)))
+        def _():
+            pltpu.make_async_remote_copy(
+                src_ref=outgoing.at[0],
+                dst_ref=arrived.at[i],
+                send_sem=send_sem.at[0],
+                recv_sem=recv_sem.at[i],
+                device_id=(i, giver),
+                device_id_type=pl.DeviceIdType.MESH,
+            ).wait_recv()
+
+    total = arrived[0]
+    for i in range(1, n_chan):
+        total = total + arrived[i]
+    out_ref[...] = total * scale
+
+    for r in range(owners):
+        for b in range(n_time):
+            mine = (time * owners + r == chan) & (time == b)
+
+            @pl.when(jnp.logical_not(mine))
+            def _():
+                copy(r * n_time + b, r, b).wait_send()
+
+
+def sum_to_owners(part, n_chan, n_time, scale):
+    count, lag_count = part.shape
+    owners = n_chan // n_time
+    block, lags = count // owners, lag_count // n_time
+    return pl.pallas_call(
+        functools.partial(sum_kernel, scale),
+        out_shape=jax.ShapeDtypeStruct((block, lags), jnp.float32),
+        in_specs=[pl.BlockSpec(memory_space=pltpu.VMEM)],
+        out_specs=pl.BlockSpec(memory_space=pltpu.VMEM),
+        scratch_shapes=[
+            pltpu.VMEM((owners * n_time, block, lags), jnp.float32),
+            pltpu.VMEM((n_chan, block, lags), jnp.float32),
+            pltpu.SemaphoreType.DMA((owners * n_time,)),
+            pltpu.SemaphoreType.DMA((n_chan,)),
+        ],
+        compiler_params=pltpu.CompilerParams(
+            collective_id=0, has_side_effects=True, vmem_limit_bytes=VMEM_LIMIT
+        ),
+        name="sum_to_owners",
+    )(part)
 
 
 def on_device(templates, record, record_tail):
@@ -179,23 +277,8 @@
     own = jnp.transpose(record)
     full_time = lax.all_gather(own, "ta", axis=0, tiled=True)
     trace = jnp.concatenate([full_time, jnp.transpose(record_tail)], axis=0)
-    lag_count = full_time.shape[0]
-    partial_value = jnp.transpose(correlate(unit, trace, lag_count))
-    here = partial_value.shape[0]
-    count_all = here * n_time
-    lag_dev = lag_count // n_time
-    placed = lax.dynamic_update_slice(
-        jnp.zeros((count_all, lag_count), jnp.float32),
-        partial_value,
-        (lax.axis_index("ta") * here, 0),
-    )
-    arranged = (
-        placed.reshape(n_chan, count_all // n_chan, n_time, lag_dev)
-        .transpose(0, 2, 1, 3)
-        .reshape(n_chan * n_time, count_all // n_chan, lag_dev)
-    )
-    stacked = lax.psum_scatter(arranged, ("ch", "ta"), scatter_dimension=0, tiled=True)[0]
-    return stacked * (1.0 / (n_chan * record.shape[0]))
+    part = correlate(unit, trace, full_time.shape[0])
+    return sum_to_owners(part, n_chan, n_time, 1.0 / (n_chan * record.shape[0]))
 
 
 def solution(mesh):

time: 242 us -> 120 us (0.50)
  waiting for transfers between devices: 125 us -> 10.7 us
  Pallas kernels: 95.5 us -> 88.7 us
    unnamed x3 -> x1, waiting for transfers between devices: 125 us -> 0.02 us
    pallas_call x1, Pallas kernels: 29.8 us -> 13.7 us  [normalize(): pl.pallas_call(normalize_kernel, grid=(channels // tile, per_tile, count...]
    all_gather x1, waiting for transfers between devices: 0.01 us -> 10.7 us  [on_device(): full_time = lax.all_gather(own, 'ta', axis=0, tiled=True)]
    pallas_call x0 -> x1, Pallas kernels: none -> 8.23 us  [sum_to_owners(): pl.pallas_call(functools.partial(sum_kernel, scale), out_shape=jax.ShapeD...]
  transfers between devices with their start and end apart: 2 -> 1, of which waited for: 1 -> 1; matrix products, arithmetic and copies ran while one was open for 0% -> 0% of each run, Pallas kernels for 12% -> 12%
where the time goes in v2:
time: 120 us; the launch traced here: 119 us
  Pallas kernels  88.7 us (74%)
  between operations  13.4 us (11%)
  waiting for transfers between devices  10.7 us (9%)
  local copies, waits for them, and re-layouts  3.32 us (3%)
  other arithmetic  2.45 us (2%)
    pallas_call x1, Pallas kernels, correlate(): pl.pallas_call(functools.partial(correlate_kernel, steps, groups, blocks)...  66.8 us
    pallas_call x1, Pallas kernels, normalize(): pl.pallas_call(normalize_kernel, grid=(channels // tile, per_tile, count...  13.7 us
    all_gather x1, waiting for transfers between devices, on_device(): full_time = lax.all_gather(own, 'ta', axis=0, tiled=True)  10.7 us
    pallas_call x1, Pallas kernels, sum_to_owners(): pl.pallas_call(functools.partial(sum_kernel, scale), out_shape=jax.ShapeD...  8.23 us
    unnamed x4, local copies, waits for them, and re-layouts  3.32 us
    concatenate x1, other arithmetic, on_device(): trace = jnp.concatenate([full_time, jnp.transpose(record_tail)], axis=0)  2.45 us
  transfers between devices with their start and end apart: 1, of which 1 were waited for; matrix products, arithmetic and copies ran while one was open for 0% of the time, Pallas kernels for 12%

profile of v2, /device:TPU:0, one launch (start us, length us, event | category | flops | bytes accessed | tf_op | source)
XLA Modules:
  0.0 118.6 jit_solution(17875443674722811864)
XLA Ops:
  6.5 0.0 all-gather.2.cloned.1.call-start
  6.5 2.0 %copy.4 = f32[512,256]{0,1:T(8,128)} copy(f32[512,256]{1,0:T(8,128)} %param.4) | data formatting | bytes 1048576 | tf_op args[1]
  8.6 0.0 all-gather.2.cloned.1.call-update
  8.6 0.0 copy-start
  8.6 13.7 %normalize_templates.1.u_ref = bf16[2,200,32,256]{3,2,1,0:T(8,128)(2,1)} custom-call(bf16[32,200,512]{2,1,0:T(8,128)(2,1)} %t_ref.1), custom_call_target="tpu_custom_call" | custom-call | tf_op jit(solution)/shard_map/normalize_templates/pallas_call | solution.py:43
  22.3 10.7 %all-gather.2.cloned.1.call-done = f32[512,512]{1,0:T(8,128)} async-done(((f32[256,512]{1,0:T(8,128)}), f32[512,512]{1,0:T(8,128)}) %all-gather.2.cloned.1.call-update) | async-done | bytes 1048592 | tf_op jit(solution)/shard_map/all_gather | solution.py:278
  32.9 0.0 copy-done
  32.9 2.5 %pad_maximum_fusion.x_ref = f32[711,512]{1,0:T(8,128)} fusion(f32[199,512]{1,0:T(8,128)S(1)} %bitcast.3, f32[512,512]{1,0:T(8,128)} %all-gather.2.cloned.1.call-done), kind=kLoop, calls=%fused_computation | loop fusion | flops 364032 | bytes 2912256 | tf_op jit(solution)/shard_map/concatenate | solution.py:279
  35.4 66.8 %correlate_windows.1.part_ref = f32[32,512]{1,0:T(8,128)} custom-call(f32[711,512]{1,0:T(8,128)} %pad_maximum_fusion.x_ref, bf16[2,200,32,256]{3,2,1,0:T(8,128)(2,1)} %normalize_templates.1.u_ref), custom_call_target="tpu_custom_call" | custom-call | tf_op jit(solution)/shard_map/correlate_windows/pallas_call | solution.py:146
  102.2 8.2 %sum_to_owners.1 = f32[4,256]{1,0:T(4,128)} custom-call(f32[32,512]{1,0:T(8,128)} %correlate_windows.1.part_ref), custom_call_target="tpu_custom_call" | custom-call | tf_op jit(solution)/shard_map/sum_to_owners/pallas_call | solution.py:254
  110.4 1.3 %copy.6 = f32[4,256]{1,0:T(4,128)} copy(f32[4,256]{1,0:T(4,128)} %sum_to_owners.1) | data formatting | bytes 8192
Async XLA Ops:
  6.5 26.4 %all-gather.2.cloned.1.call-start = ((), (), s32[]{:S(2)}) async-start(), calls=%async_computation | async-start | bytes 1572864 | tf_op jit(solution)/shard_map/all_gather | solution.py:278
  8.6 24.3 %copy-start = (f32[512,199]{0,1:T(8,128)S(1)}, f32[512,199]{0,1:T(8,128)}, u32[]{:S(2)}) copy-start(f32[512,199]{0,1:T(8,128)} %param.5) | copy-start | bytes 1222660
Sparse Core Ops, SparseCore 0:
  8.9 23.9 all-gather.1

commit v3 on v2

--- a/solution.py
+++ b/solution.py
@@ -13,8 +13,39 @@
 VMEM_LIMIT = 56 * 1024 * 1024
 
 
-def normalize_kernel(t_ref, u_ref, wide):
+def prepare_kernel(last, t_ref, rec_ref, tail_ref, u_ref, trace_ref, wide, slabs, send_sem, recv_sem):
+    n_time = lax.axis_size("ta")
+    time = lax.axis_index("ta")
     rows, samples, _ = t_ref.shape
+    lags = rec_ref.shape[1]
+    step = (pl.program_id(0) * pl.num_programs(1) + pl.program_id(1)) * pl.num_programs(
+        2
+    ) + pl.program_id(2)
+
+    def copy(i):
+        return pltpu.make_async_remote_copy(
+            src_ref=slabs.at[time],
+            dst_ref=slabs.at[time],
+            send_sem=send_sem.at[i - 1],
+            recv_sem=recv_sem.at[i - 1],
+            device_id={"ta": lax.rem(time + i, n_time)},
+            device_id_type=pl.DeviceIdType.MESH,
+        )
+
+    @pl.when(step == 0)
+    def _():
+        barrier = pltpu.get_barrier_semaphore()
+        for i in range(1, n_time):
+            pl.semaphore_signal(
+                barrier,
+                inc=1,
+                device_id={"ta": lax.rem(time + i, n_time)},
+                device_id_type=pl.DeviceIdType.MESH,
+            )
+        slabs[time] = jnp.transpose(rec_ref[...])
+        pl.semaphore_wait(barrier, n_time - 1)
+        for i in range(1, n_time):
+            copy(i).start()
 
     def one(k, carry):
         values = t_ref[k].astype(jnp.float32)
@@ -35,21 +66,51 @@
 
     lax.fori_loop(0, samples // SHIFTS, cast, 0, unroll=5)
 
-
-def normalize(templates, tile):
+    @pl.when(step == last)
+    def _():
+        trace_ref[pl.ds(n_time * lags, tail_ref.shape[0]), :] = tail_ref[...]
+        for i in range(1, n_time):
+            copy(i).wait_recv()
+        for i in range(n_time):
+            trace_ref[pl.ds(i * lags, lags), :] = slabs[i]
+        for i in range(1, n_time):
+            copy(i).wait_send()
+
+
+def prepare(templates, record, tail, n_time, tile):
     count, samples, channels = templates.shape
+    lags = record.shape[1]
+    span = n_time * lags + tail.shape[0]
     rows = math.gcd(count, 16)
     per_tile = tile // LANES
+    grid = (channels // tile, per_tile, count // rows)
     return pl.pallas_call(
-        normalize_kernel,
-        grid=(channels // tile, per_tile, count // rows),
-        in_specs=[pl.BlockSpec((rows, samples, LANES), lambda i, h, r: (r, 0, i * per_tile + h))],
-        out_specs=pl.BlockSpec((1, samples, rows, LANES), lambda i, h, r: (i, 0, r, h)),
-        out_shape=jax.ShapeDtypeStruct((channels // tile, samples, count, tile), jnp.bfloat16),
-        scratch_shapes=[pltpu.VMEM((samples * rows, LANES), jnp.float32)],
-        compiler_params=pltpu.CompilerParams(vmem_limit_bytes=VMEM_LIMIT),
-        name="normalize_templates",
-    )(templates)
+        functools.partial(prepare_kernel, math.prod(grid) - 1),
+        grid=grid,
+        in_specs=[
+            pl.BlockSpec((rows, samples, LANES), lambda i, h, r: (r, 0, i * per_tile + h)),
+            pl.BlockSpec(record.shape, lambda i, h, r: (0, 0)),
+            pl.BlockSpec(tail.shape, lambda i, h, r: (0, 0)),
+        ],
+        out_specs=[
+            pl.BlockSpec((1, samples, rows, LANES), lambda i, h, r: (i, 0, r, h)),
+            pl.BlockSpec((span, channels), lambda i, h, r: (0, 0)),
+        ],
+        out_shape=[
+            jax.ShapeDtypeStruct((channels // tile, samples, count, tile), jnp.bfloat16),
+            jax.ShapeDtypeStruct((span, channels), jnp.float32),
+        ],
+        scratch_shapes=[
+            pltpu.VMEM((samples * rows, LANES), jnp.float32),
+            pltpu.VMEM((n_time, lags, channels), jnp.float32),
+            pltpu.SemaphoreType.DMA((n_time - 1,)),
+            pltpu.SemaphoreType.DMA((n_time - 1,)),
+        ],
+        compiler_params=pltpu.CompilerParams(
+            collective_id=1, has_side_effects=True, vmem_limit_bytes=VMEM_LIMIT
+        ),
+        name="prepare",
+    )(templates, record, tail)
 
 
 def merge(left, right, n_left, n_right):
@@ -77,61 +138,61 @@
         length *= 2
 
 
-def correlate_kernel(steps, groups, blocks, x_ref, u_ref, out_ref, xs, mu, rs, w_even, w_odd, acc):
-    step = pl.program_id(0)
+def correlate_kernel(groups, blocks, x_ref, u_ref, out_ref, xs, mu, rs, w_even, w_odd):
     rows = w_even.shape[0]
     tile = x_ref.shape[1]
     lag_count = mu.shape[0]
     samples = groups * SHIFTS
     reach = xs.shape[1]
-    now = jnp.minimum(step, steps - 1)
-    before = jnp.maximum(step - 1, 0)
-    block_now = lax.rem(now // groups, blocks)
-    block_before = lax.rem(before // groups, blocks)
-    first_row = pl.multiple_of(block_now * rows, rows)
-    x_row = first_row + lax.rem(now, groups) * SHIFTS
-
-    @pl.when(step == 0)
+    steps = groups * blocks
+
+    @pl.when(pl.program_id(0) == 0)
     def _():
-        acc[...] = jnp.zeros_like(acc)
-        w_odd[...] = jnp.zeros_like(w_odd)
-
-    @pl.when(lax.rem(step, groups * blocks) == 0)
-    def _():
-        x = x_ref[...]
-        mean, var = window_stats(x, samples, lag_count)
-        mu[...] = mean
-        rs[...] = lax.rsqrt(var + 1e-06) * (1.0 / math.sqrt(samples))
-        for j in range(SHIFTS):
-            xs[j] = x[j : j + reach]
-
-    def work(w_now, w_before):
+        out_ref[...] = jnp.zeros_like(out_ref)
+
+    x = x_ref[...]
+    mean, var = window_stats(x, samples, lag_count)
+    mu[...] = mean
+    rs[...] = lax.rsqrt(var + 1e-06) * (1.0 / math.sqrt(samples))
+    for j in range(SHIFTS):
+        xs[j] = x[j : j + reach]
+
+    def build(step, w):
+        first_row = pl.multiple_of((step // groups) * rows, rows)
+        x_row = first_row + lax.rem(step, groups) * SHIFTS
         chunk = math.gcd(rows, 32)
-        weights = jnp.concatenate([u_ref[0, j] for j in range(SHIFTS)], axis=1)
-        acc_lags = pl.ds(pl.multiple_of(block_before * rows, rows), rows)
-        acc[:, acc_lags] += lax.dot_general(
-            weights, w_before[...], (((1,), (1,)), ((), ())), preferred_element_type=jnp.float32
-        )
         for r in range(0, rows, chunk):
             mean = mu[pl.ds(first_row + r, chunk), :]
             scale = rs[pl.ds(first_row + r, chunk), :]
             for j in range(SHIFTS):
                 values = xs[j, pl.ds(pl.multiple_of(x_row + r, 8), chunk), :]
-                w_now[pl.ds(r, chunk), pl.ds(j * tile, tile)] = (
-                    (values - mean) * scale
-                ).astype(jnp.bfloat16)
-
-    @pl.when(lax.rem(step, 2) == 0)
-    def _():
-        work(w_even, w_odd)
-
-    @pl.when(lax.rem(step, 2) == 1)
-    def _():
-        work(w_odd, w_even)
-
-    @pl.when(step == steps)
-    def _():
-        out_ref[...] = acc[...]
+                w[pl.ds(r, chunk), pl.ds(j * tile, tile)] = ((values - mean) * scale).astype(
+                    jnp.bfloat16
+                )
+
+    def multiply(step, w):
+        first_row = pl.multiple_of((step // groups) * rows, rows)
+        first = lax.rem(step, groups) * SHIFTS
+        weights = jnp.concatenate([u_ref[0, first + j] for j in range(SHIFTS)], axis=1)
+        out_ref[:, pl.ds(first_row, rows)] += lax.dot_general(
+            weights, w[...], (((1,), (1,)), ((), ())), preferred_element_type=jnp.float32
+        )
+
+    build(jnp.int32(0), w_even)
+
+    def pair(i, carry):
+        multiply(2 * i, w_even)
+        build(2 * i + 1, w_odd)
+        multiply(2 * i + 1, w_odd)
+        build(2 * i + 2, w_even)
+        return carry
+
+    pairs = (steps - 1) // 2
+    lax.fori_loop(0, pairs, pair, 0)
+    multiply(jnp.int32(2 * pairs), w_even)
+    if 2 * pairs + 1 < steps:
+        build(jnp.int32(steps - 1), w_odd)
+        multiply(jnp.int32(steps - 1), w_odd)
 
 
 def correlate(unit, trace, lag_count):
@@ -139,26 +200,15 @@
     span = trace.shape[0]
     groups = samples // SHIFTS
     rows = math.gcd(lag_count, 512)
-    blocks = lag_count // rows
-    steps = tiles * blocks * groups
-    per_tile = blocks * groups
     reach = lag_count + samples - SHIFTS
     return pl.pallas_call(
-        functools.partial(correlate_kernel, steps, groups, blocks),
-        grid=(steps + 1,),
+        functools.partial(correlate_kernel, groups, lag_count // rows),
+        grid=(tiles,),
         in_specs=[
-            pl.BlockSpec((span, tile), lambda s: (0, jnp.minimum(s, steps - 1) // per_tile)),
-            pl.BlockSpec(
-                (1, SHIFTS, count, tile),
-                lambda s: (
-                    jnp.maximum(s - 1, 0) // per_tile,
-                    lax.rem(jnp.maximum(s - 1, 0), groups),
-                    0,
-                    0,
-                ),
-            ),
-        ],
-        out_specs=pl.BlockSpec((count, lag_count), lambda s: (0, 0)),
+            pl.BlockSpec((span, tile), lambda i: (0, i)),
+            pl.BlockSpec((1, samples, count, tile), lambda i: (i, 0, 0, 0)),
+        ],
+        out_specs=pl.BlockSpec((count, lag_count), lambda i: (0, 0)),
         out_shape=jax.ShapeDtypeStruct((count, lag_count), jnp.float32),
         scratch_shapes=[
             pltpu.VMEM((SHIFTS, reach, tile), jnp.float32),
@@ -166,7 +216,6 @@
             pltpu.VMEM((lag_count, tile), jnp.float32),
             pltpu.VMEM((rows, SHIFTS * tile), jnp.bfloat16),
             pltpu.VMEM((rows, SHIFTS * tile), jnp.bfloat16),
-            pltpu.VMEM((count, lag_count), jnp.float32),
         ],
         compiler_params=pltpu.CompilerParams(vmem_limit_bytes=VMEM_LIMIT),
         name="correlate_windows",
@@ -273,11 +322,8 @@
     n_chan = lax.axis_size("ch")
     n_time = lax.axis_size("ta")
     tile = math.gcd(record.shape[0], 2 * LANES)
-    unit = normalize(templates, tile)
-    own = jnp.transpose(record)
-    full_time = lax.all_gather(own, "ta", axis=0, tiled=True)
-    trace = jnp.concatenate([full_time, jnp.transpose(record_tail)], axis=0)
-    part = correlate(unit, trace, full_time.shape[0])
+    unit, trace = prepare(templates, record, jnp.transpose(record_tail), n_time, tile)
+    part = correlate(unit, trace, record.shape[1] * n_time)
     return sum_to_owners(part, n_chan, n_time, 1.0 / (n_chan * record.shape[0]))
 
 

time: 120 us -> 83.2 us (0.69)
  between operations: 13.4 us -> 0.02 us
  waiting for transfers between devices: 10.7 us -> 0 us
  Pallas kernels: 88.7 us -> 81.6 us
  other arithmetic: 2.45 us -> 0 us
  local copies, waits for them, and re-layouts: 3.32 us -> 1.26 us
    all_gather x1 -> x0, waiting for transfers between devices: 10.7 us -> none  [on_device(): full_time = lax.all_gather(own, 'ta', axis=0, tiled=True)]
    pallas_call x2, Pallas kernels: 80.5 us -> 72.2 us  [the longest x1 54.3 us: correlate(): pl.pallas_call(functools.partial(correlate_kernel, groups, lag_count // r...]
    concatenate x1 -> x0, other arithmetic: 2.45 us -> none  [on_device(): trace = jnp.concatenate([full_time, jnp.transpose(record_tail)], axis=0)]
    unnamed x4 -> x1, local copies, waits for them, and re-layouts: 3.32 us -> 1.26 us
  transfers between devices with their start and end apart: 1 -> 0, of which waited for: 1 -> 0; matrix products, arithmetic and copies ran while one was open for 0% -> 0% of each run, Pallas kernels for 12% -> 0%
where the time goes in v3:
time: 83.2 us; the launch traced here: 82.9 us
  Pallas kernels  81.6 us (98%)
  local copies, waits for them, and re-layouts  1.26 us (2%)
    pallas_call x1, Pallas kernels, correlate(): pl.pallas_call(functools.partial(correlate_kernel, groups, lag_count // r...  54.3 us
    pallas_call x1, Pallas kernels, prepare(): pl.pallas_call(functools.partial(prepare_kernel, math.prod(grid) - 1), gr...  18 us
    pallas_call x1, Pallas kernels, sum_to_owners(): pl.pallas_call(functools.partial(sum_kernel, scale), out_shape=jax.ShapeD...  9.34 us

profile of v3, /device:TPU:0, one launch (start us, length us, event | category | flops | bytes accessed | tf_op | source)
XLA Modules:
  0.0 82.9 jit_solution(2036156295475515235)
XLA Ops:
  0.0 18.0 %prepare.1 = (bf16[2,200,32,256]{3,2,1,0:T(8,128)(2,1)}, f32[711,512]{1,0:T(8,128)}) custom-call(bf16[32,200,512]{2,1,0:T(8,128)(2,1)} %t_ref.1, f32[512,256]{1,0:T(8,128)} %rec_ref.1, f32[199,512]{1,0:T(8,128)} %bitcast.1), custom_call_target="tpu_custom_call" | custom-call | tf_op jit(solution)/shard_map/prepare/pallas_call | solution.py:87
  18.0 54.3 %correlate_windows.1.part_ref = f32[32,512]{1,0:T(8,128)} custom-call(f32[711,512]{1,0:T(8,128)} %get-tuple-element.7.x_ref, bf16[2,200,32,256]{3,2,1,0:T(8,128)(2,1)} %get-tuple-element.8.u_ref), custom_call_target="tpu_custom_call" | custom-call | tf_op jit(solution)/shard_map/correlate_windows/pallas_call | solution.py:204
  72.2 9.3 %sum_to_owners.1 = f32[4,256]{1,0:T(4,128)} custom-call(f32[32,512]{1,0:T(8,128)} %correlate_windows.1.part_ref), custom_call_target="tpu_custom_call" | custom-call | tf_op jit(solution)/shard_map/sum_to_owners/pallas_call | solution.py:303
  81.6 1.3 %copy.5 = f32[4,256]{1,0:T(4,128)} copy(f32[4,256]{1,0:T(4,128)} %sum_to_owners.1) | data formatting | bytes 8192

commit v4 on v3

--- a/solution.py
+++ b/solution.py
@@ -138,7 +138,7 @@
         length *= 2
 
 
-def correlate_kernel(groups, blocks, x_ref, u_ref, out_ref, xs, mu, rs, w_even, w_odd):
+def correlate_kernel(groups, blocks, x_ref, u_ref, out_ref, xs, mu, rs, w_even, w_odd, early):
     rows = w_even.shape[0]
     tile = x_ref.shape[1]
     lag_count = mu.shape[0]
@@ -149,6 +149,7 @@
     @pl.when(pl.program_id(0) == 0)
     def _():
         out_ref[...] = jnp.zeros_like(out_ref)
+        early[...] = jnp.zeros_like(early)
 
     x = x_ref[...]
     mean, var = window_stats(x, samples, lag_count)
@@ -157,11 +158,15 @@
     for j in range(SHIFTS):
         xs[j] = x[j : j + reach]
 
-    def build(step, w):
+    half = rows // 2
+    chunk = math.gcd(rows, 32)
+    slices = math.gcd(4, rows // chunk)
+    per_slice = SHIFTS // slices
+
+    def build(step, w, part):
         first_row = pl.multiple_of((step // groups) * rows, rows)
         x_row = first_row + lax.rem(step, groups) * SHIFTS
-        chunk = math.gcd(rows, 32)
-        for r in range(0, rows, chunk):
+        for r in range(part * (rows // slices), (part + 1) * (rows // slices), chunk):
             mean = mu[pl.ds(first_row + r, chunk), :]
             scale = rs[pl.ds(first_row + r, chunk), :]
             for j in range(SHIFTS):
@@ -170,29 +175,53 @@
                     jnp.bfloat16
                 )
 
-    def multiply(step, w):
-        first_row = pl.multiple_of((step // groups) * rows, rows)
-        first = lax.rem(step, groups) * SHIFTS
-        weights = jnp.concatenate([u_ref[0, first + j] for j in range(SHIFTS)], axis=1)
-        out_ref[:, pl.ds(first_row, rows)] += lax.dot_general(
-            weights, w[...], (((1,), (1,)), ((), ())), preferred_element_type=jnp.float32
-        )
-
-    build(jnp.int32(0), w_even)
+    def multiply(step, w, part):
+        first = lax.rem(step, groups) * SHIFTS + part * per_slice
+        weights = jnp.concatenate([u_ref[0, first + j] for j in range(per_slice)], axis=1)
+        depth = pl.ds(part * per_slice * tile, per_slice * tile)
+        contract = (((1,), (1,)), ((), ()))
+        left = lax.dot_general(
+            w[pl.ds(0, half), depth], weights, contract, preferred_element_type=jnp.float32
+        )
+        right = lax.dot_general(
+            weights, w[pl.ds(half, half), depth], contract, preferred_element_type=jnp.float32
+        )
+        return left, right
+
+    def both(step, w, next_step, w_next):
+        left, right = None, None
+        for part in range(slices):
+            if w is not None:
+                more_left, more_right = multiply(step, w, part)
+                left = more_left if left is None else left + more_left
+                right = more_right if right is None else right + more_right
+            if w_next is not None:
+                build(next_step, w_next, part)
+        if w is not None:
+            block = step // groups
+            first_row = pl.multiple_of(block * rows, rows)
+            early[pl.ds(pl.multiple_of(block * half, half), half), :] += left
+            out_ref[:, pl.ds(first_row + half, half)] += right
+
+    both(None, None, jnp.int32(0), w_even)
 
     def pair(i, carry):
-        multiply(2 * i, w_even)
-        build(2 * i + 1, w_odd)
-        multiply(2 * i + 1, w_odd)
-        build(2 * i + 2, w_even)
+        both(2 * i, w_even, 2 * i + 1, w_odd)
+        both(2 * i + 1, w_odd, 2 * i + 2, w_even)
         return carry
 
     pairs = (steps - 1) // 2
     lax.fori_loop(0, pairs, pair, 0)
-    multiply(jnp.int32(2 * pairs), w_even)
     if 2 * pairs + 1 < steps:
-        build(jnp.int32(steps - 1), w_odd)
-        multiply(jnp.int32(steps - 1), w_odd)
+        both(jnp.int32(2 * pairs), w_even, jnp.int32(steps - 1), w_odd)
+        both(jnp.int32(steps - 1), w_odd, None, None)
+    else:
+        both(jnp.int32(2 * pairs), w_even, None, None)
+
+    @pl.when(pl.program_id(0) == pl.num_programs(0) - 1)
+    def _():
+        for i in range(blocks):
+            out_ref[:, pl.ds(i * rows, half)] = jnp.transpose(early[pl.ds(i * half, half), :])
 
 
 def correlate(unit, trace, lag_count):
@@ -216,6 +245,7 @@
             pltpu.VMEM((lag_count, tile), jnp.float32),
             pltpu.VMEM((rows, SHIFTS * tile), jnp.bfloat16),
             pltpu.VMEM((rows, SHIFTS * tile), jnp.bfloat16),
+            pltpu.VMEM((lag_count // 2, count), jnp.float32),
         ],
         compiler_params=pltpu.CompilerParams(vmem_limit_bytes=VMEM_LIMIT),
         name="correlate_windows",

time: 83.2 us -> 81.7 us (0.982)
  Pallas kernels: 81.6 us -> 80.1 us
    pallas_call x1, Pallas kernels: 54.3 us -> 52.8 us  [correlate(): pl.pallas_call(functools.partial(correlate_kernel, groups, lag_count // r...]
where the time goes in v4:
time: 81.7 us; the launch traced here: 81.4 us
  Pallas kernels  80.1 us (98%)
  local copies, waits for them, and re-layouts  1.26 us (2%)
    pallas_call x1, Pallas kernels, correlate(): pl.pallas_call(functools.partial(correlate_kernel, groups, lag_count // r...  52.8 us
    pallas_call x1, Pallas kernels, prepare(): pl.pallas_call(functools.partial(prepare_kernel, math.prod(grid) - 1), gr...  18 us
    pallas_call x1, Pallas kernels, sum_to_owners(): pl.pallas_call(functools.partial(sum_kernel, scale), out_shape=jax.ShapeD...  9.33 us

profile of v4, /device:TPU:0, one launch (start us, length us, event | category | flops | bytes accessed | tf_op | source)
XLA Modules:
  0.0 81.4 jit_solution(12184980253838828308)
XLA Ops:
  0.0 18.0 %prepare.1 = (bf16[2,200,32,256]{3,2,1,0:T(8,128)(2,1)}, f32[711,512]{1,0:T(8,128)}) custom-call(bf16[32,200,512]{2,1,0:T(8,128)(2,1)} %t_ref.1, f32[512,256]{1,0:T(8,128)} %rec_ref.1, f32[199,512]{1,0:T(8,128)} %bitcast.1), custom_call_target="tpu_custom_call" | custom-call | tf_op jit(solution)/shard_map/prepare/pallas_call | solution.py:87
  18.0 52.8 %correlate_windows.1.part_ref = f32[32,512]{1,0:T(8,128)} custom-call(f32[711,512]{1,0:T(8,128)} %get-tuple-element.7.x_ref, bf16[2,200,32,256]{3,2,1,0:T(8,128)(2,1)} %get-tuple-element.8.u_ref), custom_call_target="tpu_custom_call" | custom-call | tf_op jit(solution)/shard_map/correlate_windows/pallas_call | solution.py:233
  70.7 9.3 %sum_to_owners.1 = f32[4,256]{1,0:T(4,128)} custom-call(f32[32,512]{1,0:T(8,128)} %correlate_windows.1.part_ref), custom_call_target="tpu_custom_call" | custom-call | tf_op jit(solution)/shard_map/sum_to_owners/pallas_call | solution.py:333
  80.1 1.3 %copy.5 = f32[4,256]{1,0:T(4,128)} copy(f32[4,256]{1,0:T(4,128)} %sum_to_owners.1) | data formatting | bytes 8192

commit v5 on v4

--- a/solution.py
+++ b/solution.py
@@ -18,6 +18,7 @@
     time = lax.axis_index("ta")
     rows, samples, _ = t_ref.shape
     lags = rec_ref.shape[1]
+    stride = wide.shape[0] // samples
     step = (pl.program_id(0) * pl.num_programs(1) + pl.program_id(1)) * pl.num_programs(
         2
     ) + pl.program_id(2)
@@ -43,7 +44,10 @@
                 device_id_type=pl.DeviceIdType.MESH,
             )
         slabs[time] = jnp.transpose(rec_ref[...])
-        pl.semaphore_wait(barrier, n_time - 1)
+
+    @pl.when(step == min(1, last))
+    def _():
+        pl.semaphore_wait(pltpu.get_barrier_semaphore(), n_time - 1)
         for i in range(1, n_time):
             copy(i).start()
 
@@ -51,7 +55,7 @@
         values = t_ref[k].astype(jnp.float32)
         centred = values - jnp.mean(values, axis=0, keepdims=True)
         power = jnp.mean(centred * centred, axis=0, keepdims=True)
-        wide[pl.ds(k, samples, stride=rows), :] = centred * (
+        wide[pl.ds(k, samples, stride=stride), :] = centred * (
             lax.rsqrt(power + 1e-06) * (1.0 / math.sqrt(samples))
         )
         return carry
@@ -60,8 +64,9 @@
 
     def cast(i, carry):
         first = i * SHIFTS
-        part = wide[pl.ds(pl.multiple_of(first * rows, 8), SHIFTS * rows), :]
-        u_ref[0, pl.ds(first, SHIFTS)] = part.reshape(SHIFTS, rows, LANES).astype(jnp.bfloat16)
+        part = wide[pl.ds(pl.multiple_of(first * stride, 8), SHIFTS * stride), :]
+        part = part.reshape(SHIFTS, stride, LANES)[:, :rows]
+        u_ref[0, pl.ds(first, SHIFTS)] = part.astype(jnp.bfloat16)
         return carry
 
     lax.fori_loop(0, samples // SHIFTS, cast, 0, unroll=5)
@@ -101,7 +106,7 @@
             jax.ShapeDtypeStruct((span, channels), jnp.float32),
         ],
         scratch_shapes=[
-            pltpu.VMEM((samples * rows, LANES), jnp.float32),
+            pltpu.VMEM((samples * (rows + SHIFTS), LANES), jnp.float32),
             pltpu.VMEM((n_time, lags, channels), jnp.float32),
             pltpu.SemaphoreType.DMA((n_time - 1,)),
             pltpu.SemaphoreType.DMA((n_time - 1,)),
@@ -121,9 +126,17 @@
     return (a0 + w1 * gap, w0 * v0 + w1 * v1 + (w0 * w1) * (gap * gap))
 
 
-def window_stats(x, samples, lag_count):
-    mean, var, length = x, jnp.zeros_like(x), 1
-    total, done = None, 0
+def window_stats(xs, samples, lag_count):
+    mean = xs[0]
+    for j in range(1, SHIFTS):
+        mean = mean + xs[j]
+    mean = mean * (1.0 / SHIFTS)
+    var = None
+    for j in range(SHIFTS):
+        gap = xs[j] - mean
+        var = gap * gap if var is None else var + gap * gap
+    var = var * (1.0 / SHIFTS)
+    total, done, length = None, 0, SHIFTS
     while True:
         if samples & length:
             piece = (mean[done : done + lag_count], var[done : done + lag_count])
@@ -152,11 +165,11 @@
         early[...] = jnp.zeros_like(early)
 
     x = x_ref[...]
-    mean, var = window_stats(x, samples, lag_count)
+    for j in range(SHIFTS):
+        xs[j] = x[j : j + reach]
+    mean, var = window_stats(xs, samples, lag_count)
     mu[...] = mean
     rs[...] = lax.rsqrt(var + 1e-06) * (1.0 / math.sqrt(samples))
-    for j in range(SHIFTS):
-        xs[j] = x[j : j + reach]
 
     half = rows // 2
     chunk = math.gcd(rows, 32)

time: 81.7 us -> 83 us (1.016)
    pallas_call x1, Pallas kernels: 18 us -> 19 us  [prepare(): pl.pallas_call(functools.partial(prepare_kernel, math.prod(grid) - 1), gr...]
    pallas_call x1, Pallas kernels: 9.33 us -> 8.36 us  [sum_to_owners(): pl.pallas_call(functools.partial(sum_kernel, scale), out_shape=jax.ShapeD...]
where the time goes in v5:
time: 83 us; the launch traced here: 82 us
  Pallas kernels  80.7 us (97%)
  local copies, waits for them, and re-layouts  1.26 us (2%)
    pallas_call x1, Pallas kernels, correlate(): pl.pallas_call(functools.partial(correlate_kernel, groups, lag_count // r...  53.3 us
    pallas_call x1, Pallas kernels, prepare(): pl.pallas_call(functools.partial(prepare_kernel, math.prod(grid) - 1), gr...  19 us
    pallas_call x1, Pallas kernels, sum_to_owners(): pl.pallas_call(functools.partial(sum_kernel, scale), out_shape=jax.ShapeD...  8.36 us

profile of v5, /device:TPU:0, one launch (start us, length us, event | category | flops | bytes accessed | tf_op | source)
XLA Modules:
  0.0 82.0 jit_solution(9659647137703876530)
XLA Ops:
  0.0 19.0 %prepare.1 = (bf16[2,200,32,256]{3,2,1,0:T(8,128)(2,1)}, f32[711,512]{1,0:T(8,128)}) custom-call(bf16[32,200,512]{2,1,0:T(8,128)(2,1)} %t_ref.1, f32[512,256]{1,0:T(8,128)} %rec_ref.1, f32[199,512]{1,0:T(8,128)} %bitcast.1), custom_call_target="tpu_custom_call" | custom-call | tf_op jit(solution)/shard_map/prepare/pallas_call | solution.py:92
  19.0 53.3 %correlate_windows.1.part_ref = f32[32,512]{1,0:T(8,128)} custom-call(f32[711,512]{1,0:T(8,128)} %get-tuple-element.7.x_ref, bf16[2,200,32,256]{3,2,1,0:T(8,128)(2,1)} %get-tuple-element.8.u_ref), custom_call_target="tpu_custom_call" | custom-call | tf_op jit(solution)/shard_map/correlate_windows/pallas_call | solution.py:246
  72.4 8.4 %sum_to_owners.1 = f32[4,256]{1,0:T(4,128)} custom-call(f32[32,512]{1,0:T(8,128)} %correlate_windows.1.part_ref), custom_call_target="tpu_custom_call" | custom-call | tf_op jit(solution)/shard_map/sum_to_owners/pallas_call | solution.py:346
  80.7 1.3 %copy.5 = f32[4,256]{1,0:T(4,128)} copy(f32[4,256]{1,0:T(4,128)} %sum_to_owners.1) | data formatting | bytes 8192
